TPU v7x, 256 devices: a whole 4x4x8 slice. The times are simulated.
256 devices in a mesh: tm: 64 (over y, z, x_lo), grp: 4 (over x_hi, core).
Axes of the slice: x: 4 (x_hi: 2, x_lo: 2; x = x_hi * 2 + x_lo), y: 4, z: 8, core: 2. Of those that a mesh axis runs over, the one named last changes fastest.
Arguments:
- raw: bfloat16 [2, 262144], P(None, ('tm', 'grp')), may hold values from -7 to 7
- taper: float32 [1024], replicated, may hold values from 0.25 to 1.75
- seg_window: float32 [4096], replicated, may hold values from 0.25 to 1.75
Outputs:
- spectra: float32 [1024, 4096], P(('tm', 'grp'))
All inputs are finite; a program needn't handle non-finite values.
Results may differ from a plain program's by a relative error of at most 0.0011.
The roundings to bfloat16 on the way count: a program that leaves them out, or rounds other values in their place, can miss the bound.
Values may be sent and summed in bfloat16 or wider, within the bound.
A program may use at most 128 MiB of HBM per device.

v0:
```python
import math

import jax
import jax.numpy as jnp
from jax import lax
from jax.sharding import PartitionSpec as P


def with_halo(cells, sides, width):
    for axis, dim in sides:
        count = lax.axis_size(axis)
        ends = count - 1
        head = lax.slice_in_dim(cells, 0, width, axis=dim)
        tail = lax.slice_in_dim(cells, cells.shape[dim] - width, cells.shape[dim], axis=dim)
        cells = jnp.concatenate(
            [
                lax.ppermute(tail, axis, [(i, (i + 1) % count) for i in range(ends)]),
                cells,
                lax.ppermute(head, axis, [((i + 1) % count, i) for i in range(ends)]),
            ],
            axis=dim,
        )
    return cells


def coefficients(channel_ids, taper):
    tap_count = taper.shape[0]
    tap_ids = jnp.arange(tap_count, dtype=jnp.int32)
    phases = channel_ids[:, None] * tap_ids[None, :] % tap_count
    angle = 2.0 * math.pi / tap_count * phases.astype(jnp.float32)
    weight = taper[None, :] / math.sqrt(tap_count)
    return (
        (weight * jnp.cos(angle)).astype(jnp.bfloat16),
        (weight * jnp.sin(angle)).astype(jnp.bfloat16),
    )


def rotation(row_count, col_count, period):
    row_ids = jnp.arange(row_count, dtype=jnp.int32)
    col_ids = jnp.arange(col_count, dtype=jnp.int32)
    angle = (
        2.0 * math.pi / period * (row_ids[:, None] * col_ids[None, :] % period).astype(jnp.float32)
    )
    return (jnp.cos(angle), jnp.sin(angle))


def transform(stacked):
    length = stacked.shape[-1]
    first_len = 2 ** ((length.bit_length() - 1) // 2)
    second = length // first_len
    leading = stacked.shape[1:-1]
    highest = lax.Precision.HIGHEST
    real_part = stacked[0].reshape(leading + (first_len, second))
    imag_part = stacked[1].reshape(leading + (first_len, second))
    cos_first, sin_first = rotation(first_len, first_len, first_len)
    section_re = jnp.einsum(
        "...mk,mq->...qk", real_part, cos_first, precision=highest
    ) + jnp.einsum("...mk,mq->...qk", imag_part, sin_first, precision=highest)
    section_im = jnp.einsum(
        "...mk,mq->...qk", imag_part, cos_first, precision=highest
    ) - jnp.einsum("...mk,mq->...qk", real_part, sin_first, precision=highest)
    cos_turn, sin_turn = rotation(first_len, second, length)
    turn_re = section_re * cos_turn + section_im * sin_turn
    turn_im = section_im * cos_turn - section_re * sin_turn
    cos_second, sin_second = rotation(second, second, second)
    out_re = jnp.einsum("...qm,mb->...bq", turn_re, cos_second, precision=highest) + jnp.einsum(
        "...qm,mb->...bq", turn_im, sin_second, precision=highest
    )
    out_im = jnp.einsum("...qm,mb->...bq", turn_im, cos_second, precision=highest) - jnp.einsum(
        "...qm,mb->...bq", turn_re, sin_second, precision=highest
    )
    return jnp.stack(
        [out_re.reshape(leading + (length,)), out_im.reshape(leading + (length,))]
    ) / math.sqrt(length)


def power_sum(chan_pair, samples, window, stride_len):
    seg_len = window.shape[0]
    chan_count = chan_pair.shape[1]
    frame_count = chan_pair.shape[2]
    sample_count = frame_count * stride_len
    chan_re = chan_pair[0].astype(jnp.float32)[:, :, None]
    chan_im = chan_pair[1].astype(jnp.float32)[:, :, None]
    samp_re = samples[0].astype(jnp.float32).reshape(frame_count, stride_len)
    samp_im = samples[1].astype(jnp.float32).reshape(frame_count, stride_len)
    folded = (chan_count, sample_count // seg_len, seg_len)
    prod_re = (chan_re * samp_re + chan_im * samp_im).reshape(folded) * window
    prod_im = (chan_im * samp_re - chan_re * samp_im).reshape(folded) * window
    estimate = transform(jnp.stack([prod_re, prod_im]))
    return jnp.sum(estimate[0] * estimate[0] + estimate[1] * estimate[1], axis=1)


def frames_of(extended, stride_len, tap_count, frame_count):
    pieces = extended.reshape(2, extended.shape[1] // stride_len, stride_len)
    windows = jnp.concatenate(
        [pieces[:, offset : offset + frame_count] for offset in range(tap_count // stride_len)], 2
    )
    return jnp.concatenate([windows[0], windows[1]], 1)


def body(raw, taper, seg_window):
    devices_grp = lax.axis_size("grp")
    devices_tm = lax.axis_size("tm")
    grp_index = lax.axis_index("grp")
    tap_count = taper.shape[0]
    half_taps = tap_count // 2
    stride_len = tap_count // 4
    own_count = tap_count // (devices_tm * devices_grp)
    strip_count = own_count * devices_tm
    seg_len = seg_window.shape[0]
    block = lax.all_gather(raw, "grp", axis=1, tiled=True)
    block_len = block.shape[1]
    frame_count = block_len // stride_len
    seg_total = devices_tm * block_len // seg_len
    extended = with_halo(block, (("tm", 1),), half_taps)
    dest_ids = jnp.arange(devices_tm, dtype=jnp.int32)
    column_ids = jnp.arange(own_count, dtype=jnp.int32)
    channel_ids = (
        (dest_ids[:, None] * devices_grp + grp_index) * own_count + column_ids[None, :]
    ).reshape(-1)
    cosine, sine = coefficients(channel_ids, taper)
    table = jnp.concatenate(
        [jnp.concatenate([cosine.T, -sine.T], 1), jnp.concatenate([sine.T, cosine.T], 1)], 0
    )
    frames = frames_of(extended, stride_len, tap_count, frame_count)
    channels = jnp.dot(frames, table, preferred_element_type=jnp.float32).astype(jnp.bfloat16)
    chan_pair = channels.T.reshape(2, strip_count, frame_count)
    sums = lax.psum_scatter(
        power_sum(chan_pair, block, seg_window, stride_len), "tm", scatter_dimension=0, tiled=True
    )
    return sums / seg_total


def solution(mesh):
    placed = (P(None, ("tm", "grp")), P(), P())
    return jax.shard_map(
        body, mesh=mesh, in_specs=placed, out_specs=P(("tm", "grp"), None), check_vma=False
    )
```

profile of v0, /device:TPU:4, one launch (start us, length us, event | category | flops | bytes accessed | tf_op | source)
XLA Modules:
  0.0 720.4 jit_solution(16988415826809122004)
XLA Ops:
  6.5 6.8 all_gather.3
  13.4 3.1 collective-permute-start
  16.5 1.3 collective-permute-start.1
  18.0 0.7 broadcast_multiply_fusion.1
  18.6 4.6 multiply_convert_fusion
  23.2 4.4 fusion.61
  28.2 0.8 mul.364
  29.7 5.2 fusion.7
  34.9 5.2 fusion.6
  40.1 5.3 fusion.38
  45.4 6.8 fusion.3
  52.2 6.4 fusion.12
  58.6 6.0 fusion.10
  64.7 6.2 add_bitcast_fusion
  70.9 2.4 copy.35
  73.3 6.1 subtract_bitcast_fusion
  79.4 2.6 copy.38
  82.6 2.5 fusion.1
  85.1 0.6 copy-done
  85.8 0.6 dynamic-slice
  87.0 622.9 %all-reduce.3.cloned.1.call-done = f32[256,4096]{0,1:T(8,128)} async-done(((f32[256,4096]{0,1:T(8,128)}), f32[256,4096]{0,1:T(8,128)}) %all-reduce.3.cloned.1.call-update) | async-done | bytes 4194320
  709.9 2.2 constant_dynamic-slice_fusion
  712.1 0.6 copy.39
  712.7 0.7 broadcast_multiply_fusion
  (28 shorter events, 1.9 us)
Async XLA Ops:
  6.5 703.3 %all-reduce.3.cloned.1.call-start = ((), (), s32[]{:S(2)}) async-start(), calls=%async_computation | async-start | bytes 8388608
  13.4 15.8 %collective-permute-start = (bf16[2,512]{1,0:T(2,128)(2,1)S(1)}, bf16[2,512]{1,0:T(2,128)(2,1)S(1)}, u32[]{:S(2)}, u32[]{:S(2)}) collective-permute-start(bf16[2,512]{1,0:T(2,128)(2,1)S(1)} %get-tuple-element.17), channel_id=1, source_target_pairs={{0,4},{4,8},{8,12},{12,16},{16,20},{20,24},{24,28},{28,32},{32,36}... | collective-permute-start | bytes 6152 | tf_op jit(solution)/shard_map/ppermute | solution.py:17
  16.5 12.7 %collective-permute-start.1 = (bf16[2,512]{1,0:T(2,128)(2,1)S(1)}, bf16[2,512]{1,0:T(2,128)(2,1)S(1)}, u32[]{:S(2)}, u32[]{:S(2)}) collective-permute-start(bf16[2,512]{1,0:T(2,128)(2,1)S(1)} %get-tuple-element.18), channel_id=1, source_target_pairs={{4,0},{8,4},{12,8},{16,12},{20,16},{24,20},{28,24},{32,28},{36,32}... | collective-permute-start | bytes 6152 | tf_op jit(solution)/shard_map/ppermute | solution.py:19
  85.1 0.7 copy-start
Sparse Core Ops, SparseCore 0:
  85.3 624.5 all-reduce.2
where the time goes:
time: 723 us; the launch traced here: 720 us
  waiting for transfers between devices  623 us (86%)
  matrix products  47.5 us (7%)
  between operations  14.5 us (2%)
  other arithmetic  13.8 us (2%)
  local copies, waits for them, and re-layouts  10.5 us (1%)
    unnamed x2, waiting for transfers between devices  623 us
  transfers between devices with their start and end apart: 3, of which 1 were waited for; matrix products, arithmetic and copies ran while one was open for 2% of the time, Pallas kernels for 0%

commit v1 on v0

v1 whole, which is shorter than its diff:
```python
import math

import jax
import jax.numpy as jnp
import numpy as np
from jax import lax
from jax.experimental import pallas as pl
from jax.experimental.pallas import tpu as pltpu
from jax.sharding import PartitionSpec as P

MESH = pl.DeviceIdType.MESH
F32 = jnp.float32
BF16 = jnp.bfloat16

CHANNELS = 1024
NFFT = 4096
STRIDE = 256
PER_SEG = NFFT // STRIDE
SEG = 64
PLANES, DEPTH, LINE = 4, 8, 8
PLANE_SEG = SEG // PLANES
ROWS = PLANE_SEG * PER_SEG
STRIP = PLANES * LINE * 4
WIDTH = NFFT // LINE


def tables():
    z = np.arange(DEPTH)[:, None, None]
    row = np.arange(STRIP)[None, :, None]
    channel = (row // 32) * 256 + z * 32 + row % 32
    phase = (channel * np.arange(CHANNELS)[None, None, :]) % CHANNELS
    angle = (np.float32(2.0 * math.pi / CHANNELS) * phase.astype(np.float32)).astype(np.float64)
    channel_table = np.concatenate([np.cos(angle), np.sin(angle)], 1).astype(np.float32)
    q = np.arange(LINE)[:, None, None] * WIDTH + np.arange(WIDTH)[None, None, :]
    turn = 2.0 * np.pi / NFFT * ((q * np.arange(STRIDE)[None, :, None]) % NFFT)
    full = np.concatenate([np.cos(turn), -np.sin(turn)], 1)
    high = full.astype(jnp.bfloat16)
    low = (full - high.astype(np.float64)).astype(jnp.bfloat16)
    turn_table = np.stack([high, low], 1)
    j = np.arange(PER_SEG)[:, None]
    step = 2.0 * np.pi / PER_SEG * ((j * np.arange(WIDTH)[None, :]) % PER_SEG)
    step_table = np.stack([np.cos(step), np.sin(step)]).astype(np.float32)
    return channel_table, turn_table, step_table


def kernel(
    raw, taper, window, step_hbm, channel_hbm, turn_hbm, out,
    tile32, tile, buf, halo, rows32, coef32, coef, turn, step, lhs, rhs, acc, blocks, landed,
    local_sem, send_sem, recv_sem,
):
    tm, grp = lax.axis_index("tm"), lax.axis_index("grp")
    y, z, x_lo = tm // 16, lax.rem(tm // 2, DEPTH), lax.rem(tm, 2)
    x_hi, core = grp // 2, lax.rem(grp, 2)
    line = x_lo * 4 + grp
    half = lax.rem(tm, 16) * 2 + x_hi
    place = y * 8 + line

    loads = [
        pltpu.make_async_copy(channel_hbm.at[z], coef32, local_sem.at[0]),
        pltpu.make_async_copy(turn_hbm.at[line], turn, local_sem.at[1]),
        pltpu.make_async_copy(step_hbm, step, local_sem.at[2]),
    ]

    def same_core(i):
        return (y * 16 + i // 2, lax.rem(i, 2) * 2 + core)

    def same_depth(i):
        return ((i // 8 * DEPTH + z) * 2 + lax.rem(i // 4, 2), lax.rem(i, 4))

    partner = (tm, x_hi * 2 + 1 - core)

    barrier = pltpu.get_barrier_semaphore()

    @pl.loop(0, 31)
    def _(i):
        to = same_core(lax.rem(half + 1 + i, 32))
        pl.semaphore_signal(barrier, inc=1, device_id=to, device_id_type=MESH)

    @pl.loop(0, 31)
    def _(i):
        to = same_depth(lax.rem(place + 1 + i, 32))
        pl.semaphore_signal(barrier, inc=1, device_id=to, device_id_type=MESH)

    for load in loads:
        load.start()

    pair = raw[...].astype(F32)
    for part in range(2):
        for chunk in range(8):
            odd, frame = chunk % 2, chunk // 2
            value = pair[part : part + 1, chunk * 128 : (chunk + 1) * 128]
            tile32[0, part * 8 + odd * 4 + frame, :] = value[0]
            tile32[1, part * 8 + (1 - odd) * 4 + frame, :] = value[0]
    tile[...] = jnp.where(core == 0, tile32[0], tile32[1]).astype(BF16)

    @pl.when(y == 0)
    def _():
        halo[0] = jnp.zeros((16, 128), BF16)

    @pl.when(y == PLANES - 1)
    def _():
        halo[1] = jnp.zeros((16, 128), BF16)

    pl.semaphore_wait(barrier, 62)

    own = core * 32 + half
    pltpu.make_async_copy(tile, buf.at[own], recv_sem.at[0]).start()

    @pl.loop(0, 31)
    def _(i):
        pltpu.make_async_remote_copy(
            tile, buf.at[own], send_sem.at[0], recv_sem.at[0],
            device_id=same_core(lax.rem(half + 1 + i, 32)), device_id_type=MESH,
        ).start()

    loads[0].wait()
    for a in range(4):
        for h in range(2):
            i = a * 2 + h
            weight = taper[i : i + 1, :] / math.sqrt(CHANNELS)
            cosine = (weight * coef32[:STRIP, i * 128 : (i + 1) * 128]).astype(BF16)
            sine = (weight * coef32[STRIP:, i * 128 : (i + 1) * 128]).astype(BF16)
            coef[a, :STRIP, h * 128 : (h + 1) * 128] = cosine
            coef[a, STRIP:, h * 128 : (h + 1) * 128] = -sine
            coef[a, :STRIP, 256 + h * 128 : 256 + (h + 1) * 128] = sine
            coef[a, STRIP:, 256 + h * 128 : 256 + (h + 1) * 128] = cosine

    mine = buf.at[pl.ds(core * 32, 32)]
    pltpu.make_async_copy(mine, mine, recv_sem.at[0]).wait()
    forward = pltpu.make_async_remote_copy(
        mine, mine, send_sem.at[1], recv_sem.at[1], device_id=partner, device_id_type=MESH
    )
    forward.start()
    forward.wait_recv()
    sent = buf.at[pl.ds(0, 31)]
    pltpu.make_async_copy(sent, sent, send_sem.at[0]).wait()

    ahead = pltpu.make_async_remote_copy(
        buf.at[63], halo.at[0], send_sem.at[2], recv_sem.at[2],
        device_id=(lax.rem(tm + 16, 64), grp), device_id_type=MESH,
    )
    behind = pltpu.make_async_remote_copy(
        buf.at[0], halo.at[1], send_sem.at[3], recv_sem.at[3],
        device_id=(lax.rem(tm + 48, 64), grp), device_id_type=MESH,
    )

    @pl.when(y < PLANES - 1)
    def _():
        ahead.start()

    @pl.when(y > 0)
    def _():
        behind.start()

    low_rows = lax.broadcasted_iota(jnp.int32, (32, 8, 128), 1) < 4
    for part in range(2):
        first = buf[0:32].astype(F32)[:, part * 8 : part * 8 + 8]
        second = buf[32:64].astype(F32)[:, part * 8 : part * 8 + 8]
        even = jnp.where(low_rows, first, second)
        odd = pltpu.roll(jnp.where(low_rows, second, first), 4, 1)
        rows32[8 : 8 + ROWS, part * 256 : part * 256 + 128] = even.reshape(ROWS, 128)
        rows32[8 : 8 + ROWS, part * 256 + 128 : part * 256 + 256] = odd.reshape(ROWS, 128)

    loads[1].wait()
    loads[2].wait()
    wins = jnp.concatenate(
        [window[pl.ds(0, PER_SEG, stride=2), :], window[pl.ds(1, PER_SEG, stride=2), :]], 1
    ) * (1.0 / 512.0)
    parts = []
    for part in range(2):
        value = rows32[8 : 8 + ROWS, part * 256 : (part + 1) * 256].reshape(PLANE_SEG, PER_SEG, STRIDE)
        parts.append((value * wins[None]).reshape(ROWS, STRIDE))
    samples = jnp.concatenate(
        [jnp.concatenate(parts, 1), jnp.concatenate([-parts[1], parts[0]], 1)], 0
    )
    high = samples.astype(BF16)
    low = (samples - high.astype(F32)).astype(BF16)
    turned = (
        jnp.dot(high, turn[0], preferred_element_type=F32)
        + jnp.dot(high, turn[1], preferred_element_type=F32)
        + jnp.dot(low, turn[0], preferred_element_type=F32)
    )
    g_re = turned[:ROWS].reshape(PLANE_SEG, PER_SEG, WIDTH)
    g_im = turned[ROWS:].reshape(PLANE_SEG, PER_SEG, WIDTH)
    cos_step, sin_step = step[0][None], step[1][None]
    for i, value in enumerate((g_re * cos_step + g_im * sin_step, g_im * cos_step - g_re * sin_step)):
        top = value.astype(BF16)
        rhs[:, i * 16 : i * 16 + 16, :] = top
        rhs[:, 32 + i * 16 : 48 + i * 16, :] = (value - top.astype(F32)).astype(BF16)

    @pl.when(y > 0)
    def _():
        ahead.wait_recv()

    @pl.when(y < PLANES - 1)
    def _():
        behind.wait_recv()

    before, after = halo[0].astype(F32), halo[1].astype(F32)
    for part in range(2):
        at = part * 256
        rows32[6:8, at : at + 128] = before[part * 8 + 6 : part * 8 + 8]
        rows32[6:8, at + 128 : at + 256] = before[part * 8 + 2 : part * 8 + 4]
        rows32[8 + ROWS : 9 + ROWS, at : at + 128] = after[part * 8 : part * 8 + 1]
        rows32[8 + ROWS : 9 + ROWS, at + 128 : at + 256] = after[part * 8 + 4 : part * 8 + 5]
    frames = jnp.zeros((ROWS, 2 * STRIP), F32)
    for a in range(4):
        frames += lax.dot_general(
            rows32[6 + a : 6 + a + ROWS, :].astype(BF16), coef[a],
            (((1,), (1,)), ((), ())), preferred_element_type=F32,
        )
    rounded = frames.astype(BF16)
    swapped = jnp.concatenate([-rounded[:, STRIP:], rounded[:, :STRIP]], 1)
    for i, value in enumerate((rounded, swapped, rounded, swapped)):
        lhs[:, i * 16 : i * 16 + 16, :] = value.reshape(PLANE_SEG, PER_SEG, 2 * STRIP)

    acc[...] = jnp.zeros_like(acc)

    @pl.loop(0, PLANE_SEG)
    def _(s):
        estimate = lax.dot_general(
            lhs[s], rhs[s], (((0,), (0,)), ((), ())), preferred_element_type=F32
        )
        acc[...] += estimate[:STRIP] * estimate[:STRIP] + estimate[STRIP:] * estimate[STRIP:]

    low_half = lax.broadcasted_iota(jnp.int32, (16, 8, 256), 1) < 4
    left = acc[:, :256].reshape(16, 8, 256)
    right = acc[:, 256:].reshape(16, 8, 256)
    even = jnp.where(low_half, left, pltpu.roll(right, 4, 1))
    odd = jnp.where(low_half, pltpu.roll(left, 4, 1), right)
    for t in range(16):
        blocks[2 * t] = even[t]
        blocks[2 * t + 1] = odd[t]

    pltpu.make_async_copy(blocks.at[place], landed.at[place], recv_sem.at[4]).start()

    @pl.loop(0, 31)
    def _(i):
        to = lax.rem(place + 1 + i, 32)
        pltpu.make_async_remote_copy(
            blocks.at[to], landed.at[place], send_sem.at[4], recv_sem.at[4],
            device_id=same_depth(to), device_id_type=MESH,
        ).start()

    pltpu.make_async_copy(landed, landed, recv_sem.at[4]).wait()
    for i in range(LINE):
        total = landed[i] + landed[8 + i] + landed[16 + i] + landed[24 + i]
        out[:, i * WIDTH : i * WIDTH + 256] = total[0:4]
        out[:, i * WIDTH + 256 : (i + 1) * WIDTH] = total[4:8]

    forward.wait_send()

    @pl.when(y < PLANES - 1)
    def _():
        ahead.wait_send()

    @pl.when(y > 0)
    def _():
        behind.wait_send()

    gone = blocks.at[pl.ds(0, 31)]
    pltpu.make_async_copy(gone, gone, send_sem.at[4]).wait()


def body(raw, taper, seg_window):
    channel_table, turn_table, step_table = tables()
    vmem = pl.BlockSpec(memory_space=pltpu.VMEM)
    hbm = pl.BlockSpec(memory_space=pl.ANY)
    return pl.pallas_call(
        kernel,
        out_shape=jax.ShapeDtypeStruct((4, NFFT), F32),
        in_specs=[vmem, vmem, vmem, hbm, hbm, hbm],
        out_specs=vmem,
        scratch_shapes=[
            pltpu.VMEM((2, 16, 128), F32),
            pltpu.VMEM((16, 128), BF16),
            pltpu.VMEM((64, 16, 128), BF16),
            pltpu.VMEM((2, 16, 128), BF16),
            pltpu.VMEM((ROWS + 16, 512), F32),
            pltpu.VMEM((2 * STRIP, CHANNELS), F32),
            pltpu.VMEM((4, 2 * STRIP, 512), BF16),
            pltpu.VMEM((2, 512, WIDTH), BF16),
            pltpu.VMEM((2, PER_SEG, WIDTH), F32),
            pltpu.VMEM((PLANE_SEG, 64, 2 * STRIP), BF16),
            pltpu.VMEM((PLANE_SEG, 64, WIDTH), BF16),
            pltpu.VMEM((STRIP, WIDTH), F32),
            pltpu.VMEM((32, 8, 256), F32),
            pltpu.VMEM((32, 8, 256), F32),
            pltpu.SemaphoreType.DMA((3,)),
            pltpu.SemaphoreType.DMA((5,)),
            pltpu.SemaphoreType.DMA((5,)),
        ],
        compiler_params=pltpu.CompilerParams(
            collective_id=0, has_side_effects=True, vmem_limit_bytes=48 * 1024 * 1024
        ),
    )(
        raw, taper.reshape(8, 128), seg_window.reshape(32, 128),
        jnp.asarray(step_table), jnp.asarray(channel_table), jnp.asarray(turn_table),
    )


def solution(mesh):
    placed = (P(None, ("tm", "grp")), P(), P())
    return jax.shard_map(
        body, mesh=mesh, in_specs=placed, out_specs=P(("tm", "grp"), None), check_vma=False
    )
```

time: 723 us -> 36.7 us (0.05)
  the two profiles are of different devices: /device:TPU:4 before, /device:TPU:1 now
where the time goes in v1:
time: 36.7 us; the launch traced here: 36.5 us
  Pallas kernels  32.9 us (90%)
  local copies, waits for them, and re-layouts  3.56 us (10%)
    pallas_call x1, Pallas kernels, body(): pl.pallas_call(kernel, out_shape=jax.ShapeDtypeStruct((4, NFFT), F32), in...  32.9 us
    unnamed x9, local copies, waits for them, and re-layouts  3.56 us

profile of v1, /device:TPU:1, one launch (start us, length us, event | category | flops | bytes accessed | tf_op | source)
XLA Modules:
  0.0 36.5 jit_solution(11245972561502473347)
XLA Ops:
  0.0 0.0 copy-start
  0.0 0.8 %copy-done = f32[2,16,512]{2,1,0:T(8,128)S(1)} copy-done((f32[2,16,512]{2,1,0:T(8,128)S(1)}, f32[2,16,512]{2,1,0:T(8,128)}, u32[]{:S(2)}) %copy-start) | copy-done | bytes 65560
  0.8 0.0 copy-start.1
  0.8 0.7 %copy-done.1 = f32[4096]{0:T(1024)S(1)} copy-done((f32[4096]{0:T(1024)S(1)}, f32[4096]{0:T(1024)}, u32[]{:S(2)}) %copy-start.1) | copy-done | bytes 16408
  1.6 0.0 copy-start.2
  1.6 0.7 %copy-done.2 = bf16[2,1024]{1,0:T(2,128)(2,1)S(1)} copy-done((bf16[2,1024]{1,0:T(2,128)(2,1)S(1)}, bf16[2,1024]{1,0:T(2,128)(2,1)}, u32[]{:S(2)}) %copy-start.2) | copy-done | bytes 4120
  2.2 0.0 copy-start.3
  2.2 0.7 %copy-done.3 = f32[1024]{0:T(1024)S(1)} copy-done((f32[1024]{0:T(1024)S(1)}, f32[1024]{0:T(1024)}, u32[]{:S(2)}) %copy-start.3) | copy-done | bytes 4120
  2.9 32.9 %shard_map.64 = f32[4,4096]{1,0:T(4,128)S(1)} custom-call(bf16[2,1024]{1,0:T(2,128)(2,1)S(1)} %copy-done.2, f32[8,128]{1,0:T(8,128)S(1)} %bitcast.3, f32[32,128]{1,0:T(8,128)S(1)} %bitcast.2, f32[2,16,512]{2,1,0:T(8,128)S(1)} %copy-done, f32[8,256,1024]{2,1,0:T(8,128)} %constant.7.clone.channel_hbm, bf16[8,2,512,512]{3,2,1,0:T(8,128)(2,1)} %constant.8.clone.turn_hbm), custom_call_target="tpu_custom_call" | custom-call | tf_op jit(solution)/shard_map/pallas_call | solution.py:269
  35.8 0.6 %copy.8 = f32[4,4096]{1,0:T(4,128)} copy(f32[4,4096]{1,0:T(4,128)S(1)} %shard_map.64) | data formatting | bytes 131072
Async XLA Ops:
  0.0 0.8 %copy-start = (f32[2,16,512]{2,1,0:T(8,128)S(1)}, f32[2,16,512]{2,1,0:T(8,128)}, u32[]{:S(2)}) copy-start(f32[2,16,512]{2,1,0:T(8,128)} %constant.6.clone.step_hbm) | copy-start | bytes 196612
  0.8 0.7 %copy-start.1 = (f32[4096]{0:T(1024)S(1)}, f32[4096]{0:T(1024)}, u32[]{:S(2)}) copy-start(f32[4096]{0:T(1024)} %param.8) | copy-start | bytes 49156
  1.6 0.7 %copy-start.2 = (bf16[2,1024]{1,0:T(2,128)(2,1)S(1)}, bf16[2,1024]{1,0:T(2,128)(2,1)}, u32[]{:S(2)}) copy-start(bf16[2,1024]{1,0:T(2,128)(2,1)} %raw.1) | copy-start | bytes 12292
  2.2 0.7 %copy-start.3 = (f32[1024]{0:T(1024)S(1)}, f32[1024]{0:T(1024)}, u32[]{:S(2)}) copy-start(f32[1024]{0:T(1024)} %param.7) | copy-start | bytes 12292

commit v2 on v1

v2 whole, which is shorter than its diff:
```python
import math

import jax
import jax.numpy as jnp
import numpy as np
from jax import lax
from jax.experimental import pallas as pl
from jax.experimental.pallas import tpu as pltpu
from jax.sharding import PartitionSpec as P

MESH = pl.DeviceIdType.MESH
F32 = jnp.float32
BF16 = jnp.bfloat16

CHANNELS = 1024
NFFT = 4096
STRIDE = 256
PER_SEG = NFFT // STRIDE
SEG = 64
PLANES, DEPTH, LINE = 4, 8, 8
PLANE_SEG = SEG // PLANES
ROWS = PLANE_SEG * PER_SEG
HALF_ROWS = ROWS // 2
STRIP = PLANES * LINE * 4
WIDTH = NFFT // LINE
HOPS = (0, 1, 2, 1)
MEMBERS = sorted(((dx, dc) for dx in range(4) for dc in range(2) if dx or dc), key=lambda m: -HOPS[m[0]])
OWNERS = sorted(
    ((dy, dx, dc) for dy in range(4) for dx in range(4) for dc in range(2) if dy or dx or dc),
    key=lambda m: -(HOPS[m[0]] + HOPS[m[1]]),
)


def tables():
    z = np.arange(DEPTH)[:, None, None]
    row = np.arange(STRIP)[None, :, None]
    channel = (row // 32) * 256 + z * 32 + row % 32
    phase = (channel * np.arange(CHANNELS)[None, None, :]) % CHANNELS
    angle = (np.float32(2.0 * math.pi / CHANNELS) * phase.astype(np.float32)).astype(np.float64)
    channel_table = np.concatenate([np.cos(angle), np.sin(angle)], 1).astype(np.float32)
    q = np.arange(LINE)[:, None, None] * WIDTH + np.arange(WIDTH)[None, None, :]
    turn = 2.0 * np.pi / NFFT * ((q * np.arange(STRIDE)[None, :, None]) % NFFT)
    full = np.concatenate([np.cos(turn), -np.sin(turn)], 1)
    high = full.astype(jnp.bfloat16)
    low = (full - high.astype(np.float64)).astype(jnp.bfloat16)
    turn_table = np.stack([high, low], 1)
    j = np.arange(PER_SEG)[:, None]
    step = 2.0 * np.pi / PER_SEG * ((j * np.arange(WIDTH)[None, :]) % PER_SEG)
    step_table = np.stack([np.cos(step), np.sin(step)]).astype(np.float32)
    return channel_table, turn_table, step_table


def kernel(
    raw_hbm, taper_hbm, window_hbm, step_hbm, channel_hbm, turn_hbm, out,
    raw, taper, window, tile32, buf, halo, rows32, coef32, coef, turn, step, lhs, rhs, acc, blocks, landed,
    local_sem, send_sem, recv_sem,
):
    tm, grp = lax.axis_index("tm"), lax.axis_index("grp")
    y, z, x_lo = tm // 16, lax.rem(tm // 2, DEPTH), lax.rem(tm, 2)
    x, core = grp // 2 * 2 + x_lo, lax.rem(grp, 2)
    line = x_lo * 4 + grp
    mine, other = z // 4, 1 - z // 4
    zz = lax.rem(z, 4)
    place = y * 8 + line

    xs = [lax.rem(x + d, 4) for d in range(4)]
    ys = [lax.rem(y + d, PLANES) for d in range(PLANES)]
    cores = [core, 1 - core]

    def member(dx, dc):
        return lax.rem(xs[dx], 2) * 4 + xs[dx] // 2 * 2 + cores[dc]

    def at(plane, depth, member):
        return ((plane * DEPTH + depth) * 2 + member // 4, lax.rem(member, 4))

    def send(src, dst, send_at, recv_at, to):
        pltpu.make_async_remote_copy(
            src, dst, send_sem.at[send_at], recv_sem.at[recv_at],
            device_id=to, device_id_type=MESH,
        ).start()

    def arrived(ref, sem):
        pltpu.make_async_copy(ref, ref, sem).wait()

    loads = [
        pltpu.make_async_copy(raw_hbm, raw, local_sem.at[0]),
        pltpu.make_async_copy(taper_hbm, taper, local_sem.at[1]),
        pltpu.make_async_copy(channel_hbm.at[z], coef32, local_sem.at[2]),
        pltpu.make_async_copy(window_hbm, window, local_sem.at[3]),
        pltpu.make_async_copy(step_hbm, step, local_sem.at[4]),
        pltpu.make_async_copy(turn_hbm.at[line], turn, local_sem.at[5]),
    ]
    loads[0].start()

    barrier = pltpu.get_barrier_semaphore()

    def greet(to):
        pl.semaphore_signal(barrier, inc=1, device_id=to, device_id_type=MESH)

    @pl.when(mine == 0)
    def _():
        for i in range(4):
            greet(at(y, 4 + i, line))

    for i in range(1, 4):
        greet(at(y, mine * 4 + lax.rem(zz + i, 4), line))

    for dx, dc in MEMBERS:
        greet(at(y, z, member(dx, dc)))
    for i in range(1, PLANES):
        greet(at(ys[i], z, line))

    for load in loads[1:]:
        load.start()

    loads[0].wait()
    pair = raw[...].astype(F32)
    for part in range(2):
        for chunk in range(8):
            odd, frame = chunk % 2, chunk // 2
            value = pair[part : part + 1, chunk * 128 : (chunk + 1) * 128]
            tile32[0, part * 8 + odd * 4 + frame, :] = value[0]
            tile32[1, part * 8 + (1 - odd) * 4 + frame, :] = value[0]
    own = (mine * 8 + line) * 4 + zz
    buf[own] = jnp.where(core == 0, tile32[0], tile32[1]).astype(BF16)

    @pl.when(y == 0)
    def _():
        halo[0] = jnp.zeros((16, 128), BF16)

    @pl.when(y == PLANES - 1)
    def _():
        halo[1] = jnp.zeros((16, 128), BF16)

    @pl.when(mine == 0)
    def _():
        pl.semaphore_wait(barrier, 13)

    @pl.when(mine == 1)
    def _():
        pl.semaphore_wait(barrier, 17)

    def along_z_far():
        for i in range(4):
            send(buf.at[own], buf.at[own], 0, 1, at(y, other * 4 + i, line))

    def along_x(part, send_at, recv_at):
        block = buf.at[pl.ds((part * 8 + line) * 4, 4)]
        for dx, dc in MEMBERS:
            send(block, block, send_at, recv_at, at(y, z, member(dx, dc)))

    def ends(part):
        @pl.when((part == 0) & (line == 0) & (y > 0))
        def _():
            for i in range(8):
                send(buf.at[0], halo.at[1], 3, 5, at(y - 1, z, i))

        @pl.when((part == 1) & (line == 7) & (y < PLANES - 1))
        def _():
            for i in range(8):
                send(buf.at[63], halo.at[0], 3, 4, at(y + 1, z, i))

    @pl.when(mine == 1)
    def _():
        along_z_far()

    for i in range(1, 4):
        send(buf.at[own], buf.at[own], 0, 0, at(y, mine * 4 + lax.rem(zz + i, 4), line))

    loads[1].wait()
    loads[2].wait()
    for a in range(4):
        for h in range(2):
            i = a * 2 + h
            weight = taper[i : i + 1, :] / math.sqrt(CHANNELS)
            cosine = (weight * coef32[:STRIP, i * 128 : (i + 1) * 128]).astype(BF16)
            sine = (weight * coef32[STRIP:, i * 128 : (i + 1) * 128]).astype(BF16)
            coef[a, :STRIP, h * 128 : (h + 1) * 128] = cosine
            coef[a, STRIP:, h * 128 : (h + 1) * 128] = -sine
            coef[a, :STRIP, 256 + h * 128 : 256 + (h + 1) * 128] = sine
            coef[a, STRIP:, 256 + h * 128 : 256 + (h + 1) * 128] = cosine

    arrived(buf.at[pl.ds(0, 3)], recv_sem.at[0])
    along_x(mine, 1, 2)
    for load in loads[3:]:
        load.wait()

    wins = jnp.concatenate(
        [window[pl.ds(0, PER_SEG, stride=2), :], window[pl.ds(1, PER_SEG, stride=2), :]], 1
    ) * (1.0 / 512.0)
    low_rows = lax.broadcasted_iota(jnp.int32, (4, 8, 128), 1) < 4

    def arrange(part):
        start = pl.multiple_of(8 + part * HALF_ROWS, 8)
        for p in range(2):
            evens, odds = [], []
            for i in range(4):
                first = buf[pl.ds((part * 8 + 2 * i) * 4, 4)].astype(F32)[:, p * 8 : p * 8 + 8]
                second = buf[pl.ds((part * 8 + 2 * i + 1) * 4, 4)].astype(F32)[:, p * 8 : p * 8 + 8]
                evens.append(jnp.where(low_rows, first, second))
                odds.append(pltpu.roll(jnp.where(low_rows, second, first), 4, 1))
            for h, pieces in enumerate((evens, odds)):
                at_lane = p * 256 + h * 128
                rows32[pl.ds(start, HALF_ROWS), at_lane : at_lane + 128] = jnp.stack(pieces, 1).reshape(HALF_ROWS, 128)

    def short_transforms(part):
        start = pl.multiple_of(8 + part * HALF_ROWS, 8)
        parts = []
        for p in range(2):
            value = rows32[pl.ds(start, HALF_ROWS), p * 256 : (p + 1) * 256].reshape(8, PER_SEG, STRIDE)
            parts.append((value * wins[None]).reshape(HALF_ROWS, STRIDE))
        samples = jnp.concatenate(
            [jnp.concatenate(parts, 1), jnp.concatenate([-parts[1], parts[0]], 1)], 0
        )
        high = samples.astype(BF16)
        low = (samples - high.astype(F32)).astype(BF16)
        turned = (
            jnp.dot(high, turn[0], preferred_element_type=F32)
            + jnp.dot(high, turn[1], preferred_element_type=F32)
            + jnp.dot(low, turn[0], preferred_element_type=F32)
        )
        g_re = turned[:HALF_ROWS].reshape(8, PER_SEG, WIDTH)
        g_im = turned[HALF_ROWS:].reshape(8, PER_SEG, WIDTH)
        cos_step, sin_step = step[0][None], step[1][None]
        for i, value in enumerate((g_re * cos_step + g_im * sin_step, g_im * cos_step - g_re * sin_step)):
            top = value.astype(BF16)
            rhs[pl.ds(part * 8, 8), i * 16 : i * 16 + 16, :] = top
            rhs[pl.ds(part * 8, 8), 32 + i * 16 : 48 + i * 16, :] = (value - top.astype(F32)).astype(BF16)

    def frames(runs):
        total = None
        for a in range(4):
            pieces = []
            for first, count in runs:
                start = pl.multiple_of(first * PER_SEG, 8)
                chunk = rows32[pl.ds(start, (count + 1) * PER_SEG), :]
                pieces.append(chunk[6 + a : 6 + a + count * PER_SEG].astype(BF16))
            term = lax.dot_general(
                jnp.concatenate(pieces, 0), coef[a], (((1,), (1,)), ((), ())), preferred_element_type=F32
            )
            total = term if total is None else total + term
        rounded = total.astype(BF16).astype(F32)
        swapped = jnp.concatenate([-rounded[:, STRIP:], rounded[:, :STRIP]], 1)
        row = 0
        for first, count in runs:
            for s in range(count):
                pair = jnp.concatenate([rounded[row : row + PER_SEG], swapped[row : row + PER_SEG]], 0)
                lhs[first + s] = jnp.concatenate([pair, pair], 0).T.astype(BF16)
                row += PER_SEG

    def power(segments, first):
        for n in range(2):
            lanes = slice(n * 256, (n + 1) * 256)
            total = None if first else acc[:, lanes]
            for s in segments:
                e = jnp.dot(lhs[s], rhs[s][:, lanes], preferred_element_type=F32)
                term = e[:STRIP] * e[:STRIP] + e[STRIP:] * e[STRIP:]
                total = term if total is None else total + term
            acc[:, lanes] = total

    arrived(buf.at[pl.ds(0, 28)], recv_sem.at[2])
    ends(mine)
    arrange(mine)
    short_transforms(mine)
    frames([(mine * 8 + 1, 6)])
    power([mine * 8 + s for s in range(1, 7)], True)

    arrived(buf.at[pl.ds(0, 4)], recv_sem.at[1])
    along_x(other, 2, 3)
    ends(other)

    @pl.when(mine == 0)
    def _():
        along_z_far()

    arrived(buf.at[pl.ds(0, 28)], recv_sem.at[3])

    @pl.when(y > 0)
    def _():
        arrived(halo.at[0], recv_sem.at[4])

    @pl.when(y < PLANES - 1)
    def _():
        arrived(halo.at[1], recv_sem.at[5])

    before, after = halo[0].astype(F32), halo[1].astype(F32)
    for p in range(2):
        lane = p * 256
        rows32[6:8, lane : lane + 128] = before[p * 8 + 6 : p * 8 + 8]
        rows32[6:8, lane + 128 : lane + 256] = before[p * 8 + 2 : p * 8 + 4]
        rows32[8 + ROWS : 9 + ROWS, lane : lane + 128] = after[p * 8 : p * 8 + 1]
        rows32[8 + ROWS : 9 + ROWS, lane + 128 : lane + 256] = after[p * 8 + 4 : p * 8 + 5]
    arrange(other)
    short_transforms(other)
    frames([(mine * 8, 1), (mine * 8 + 7, 1), (other * 8, 8)])
    power([mine * 8, mine * 8 + 7] + [other * 8 + s for s in range(8)], False)

    low_half = lax.broadcasted_iota(jnp.int32, (16, 8, 256), 1) < 4
    left = acc[:, :256].reshape(16, 8, 256)
    right = acc[:, 256:].reshape(16, 8, 256)
    even = jnp.where(low_half, left, pltpu.roll(right, 4, 1))
    odd = jnp.where(low_half, pltpu.roll(left, 4, 1), right)
    for t in range(16):
        blocks[2 * t] = even[t]
        blocks[2 * t + 1] = odd[t]

    for dy, dx, dc in OWNERS:
        to = ys[dy] * 8 + member(dx, dc)
        send(blocks.at[to], landed.at[place], 4, 6, at(ys[dy], z, member(dx, dc)))

    landed[place] = blocks[place]
    arrived(landed.at[pl.ds(0, 31)], recv_sem.at[6])
    for i in range(LINE):
        total = landed[i] + landed[8 + i] + landed[16 + i] + landed[24 + i]
        out[:, i * WIDTH : i * WIDTH + 256] = total[0:4]
        out[:, i * WIDTH + 256 : (i + 1) * WIDTH] = total[4:8]

    arrived(buf.at[pl.ds(0, 7)], send_sem.at[0])
    arrived(buf.at[pl.ds(0, 28)], send_sem.at[1])
    arrived(buf.at[pl.ds(0, 28)], send_sem.at[2])

    @pl.when((line == 0) & (y > 0))
    def _():
        arrived(buf.at[pl.ds(0, 8)], send_sem.at[3])

    @pl.when((line == 7) & (y < PLANES - 1))
    def _():
        arrived(buf.at[pl.ds(0, 8)], send_sem.at[3])

    arrived(blocks.at[pl.ds(0, 31)], send_sem.at[4])


def body(raw, taper, seg_window):
    channel_table, turn_table, step_table = tables()
    operands = (
        raw, taper.reshape(8, 128), seg_window.reshape(32, 128),
        jnp.asarray(step_table), jnp.asarray(channel_table), jnp.asarray(turn_table),
    )
    vmem = pl.BlockSpec(memory_space=pltpu.VMEM)
    hbm = pl.BlockSpec(memory_space=pltpu.HBM)
    return pl.pallas_call(
        kernel,
        out_shape=jax.ShapeDtypeStruct((4, NFFT), F32),
        in_specs=[hbm] * 6,
        out_specs=vmem,
        scratch_shapes=[
            pltpu.VMEM((2, 1024), BF16),
            pltpu.VMEM((8, 128), F32),
            pltpu.VMEM((32, 128), F32),
            pltpu.VMEM((2, 16, 128), F32),
            pltpu.VMEM((64, 16, 128), BF16),
            pltpu.VMEM((2, 16, 128), BF16),
            pltpu.VMEM((ROWS + 16, 512), F32),
            pltpu.VMEM((2 * STRIP, CHANNELS), F32),
            pltpu.VMEM((4, 2 * STRIP, 512), BF16),
            pltpu.VMEM((2, 512, WIDTH), BF16),
            pltpu.VMEM((2, PER_SEG, WIDTH), F32),
            pltpu.VMEM((PLANE_SEG, 2 * STRIP, 64), BF16),
            pltpu.VMEM((PLANE_SEG, 64, WIDTH), BF16),
            pltpu.VMEM((STRIP, WIDTH), F32),
            pltpu.VMEM((32, 8, 256), F32),
            pltpu.VMEM((32, 8, 256), F32),
            pltpu.SemaphoreType.DMA((6,)),
            pltpu.SemaphoreType.DMA((5,)),
            pltpu.SemaphoreType.DMA((7,)),
        ],
        compiler_params=pltpu.CompilerParams(
            collective_id=0, has_side_effects=True, vmem_limit_bytes=48 * 1024 * 1024
        ),
    )(*(pltpu.with_memory_space_constraint(x, pltpu.HBM) for x in operands))


def solution(mesh):
    placed = (P(None, ("tm", "grp")), P(), P())
    return jax.shard_map(
        body, mesh=mesh, in_specs=placed, out_specs=P(("tm", "grp"), None), check_vma=False
    )
```

time: 36.7 us -> 30.5 us (0.83)
  Pallas kernels: 32.9 us -> 29.4 us
  local copies, waits for them, and re-layouts: 3.56 us -> 0.63 us
    pallas_call x1, Pallas kernels: 32.9 us -> 29.4 us  [body(): pl.pallas_call(kernel, out_shape=jax.ShapeDtypeStruct((4, NFFT), F32), in...]
    unnamed x9 -> x1, local copies, waits for them, and re-layouts: 3.56 us -> 0.63 us
where the time goes in v2:
time: 30.5 us; the launch traced here: 30.1 us
  Pallas kernels  29.4 us (96%)
  local copies, waits for them, and re-layouts  0.63 us (2%)
    pallas_call x1, Pallas kernels, body(): pl.pallas_call(kernel, out_shape=jax.ShapeDtypeStruct((4, NFFT), F32), in...  29.4 us
    unnamed x1, local copies, waits for them, and re-layouts  0.63 us

profile of v2, /device:TPU:1, one launch (start us, length us, event | category | flops | bytes accessed | tf_op | source)
XLA Modules:
  0.0 30.1 jit_solution(17286033568468860229)
XLA Ops:
  0.0 29.4 %shard_map.64 = f32[4,4096]{1,0:T(4,128)S(1)} custom-call(bf16[2,1024]{1,0:T(2,128)(2,1)} %raw_hbm.1, f32[8,128]{1,0:T(8,128)} %bitcast.3, f32[32,128]{1,0:T(8,128)} %bitcast.2, f32[2,16,512]{2,1,0:T(8,128)} %constant.6.clone.step_hbm, f32[8,256,1024]{2,1,0:T(8,128)} %constant.7.clone.channel_hbm, bf16[8,2,512,512]{3,2,1,0:T(8,128)(2,1)} %constant.8.clone.turn_hbm), custom_call_target="tpu_custom_call" | custom-call | tf_op jit(solution)/shard_map/pallas_call | solution.py:341
  29.4 0.6 %copy.8 = f32[4,4096]{1,0:T(4,128)} copy(f32[4,4096]{1,0:T(4,128)S(1)} %shard_map.64) | data formatting | bytes 131072

commit v3 on v2

--- a/solution.py
+++ b/solution.py
@@ -110,9 +110,6 @@
     for i in range(1, PLANES):
         greet(at(ys[i], z, line))
 
-    for load in loads[1:]:
-        load.start()
-
     loads[0].wait()
     pair = raw[...].astype(F32)
     for part in range(2):
@@ -140,10 +137,6 @@
     def _():
         pl.semaphore_wait(barrier, 17)
 
-    def along_z_far():
-        for i in range(4):
-            send(buf.at[own], buf.at[own], 0, 1, at(y, other * 4 + i, line))
-
     def along_x(part, send_at, recv_at):
         block = buf.at[pl.ds((part * 8 + line) * 4, 4)]
         for dx, dc in MEMBERS:
@@ -162,10 +155,14 @@
 
     @pl.when(mine == 1)
     def _():
-        along_z_far()
+        for i in range(4):
+            send(buf.at[own], buf.at[own], 0, 7 + zz, at(y, i, line))
 
     for i in range(1, 4):
         send(buf.at[own], buf.at[own], 0, 0, at(y, mine * 4 + lax.rem(zz + i, 4), line))
+
+    for load in loads[1:]:
+        load.start()
 
     loads[1].wait()
     loads[2].wait()
@@ -228,16 +225,19 @@
             rhs[pl.ds(part * 8, 8), 32 + i * 16 : 48 + i * 16, :] = (value - top.astype(F32)).astype(BF16)
 
     def frames(runs):
+        pieces = []
+        for first, count in runs:
+            start = pl.multiple_of(first * PER_SEG, 16)
+            pieces.append(rows32[pl.ds(start, (count + 1) * PER_SEG), :].astype(BF16))
+        rows = jnp.concatenate(pieces, 0)
         total = None
         for a in range(4):
-            pieces = []
+            term = lax.dot_general(rows, coef[a], (((1,), (1,)), ((), ())), preferred_element_type=F32)
+            taken, row = [], 6 + a
             for first, count in runs:
-                start = pl.multiple_of(first * PER_SEG, 8)
-                chunk = rows32[pl.ds(start, (count + 1) * PER_SEG), :]
-                pieces.append(chunk[6 + a : 6 + a + count * PER_SEG].astype(BF16))
-            term = lax.dot_general(
-                jnp.concatenate(pieces, 0), coef[a], (((1,), (1,)), ((), ())), preferred_element_type=F32
-            )
+                taken.append(term[row : row + count * PER_SEG])
+                row += (count + 1) * PER_SEG
+            term = jnp.concatenate(taken, 0)
             total = term if total is None else total + term
         rounded = total.astype(BF16).astype(F32)
         swapped = jnp.concatenate([-rounded[:, STRIP:], rounded[:, :STRIP]], 1)
@@ -260,18 +260,46 @@
 
     arrived(buf.at[pl.ds(0, 28)], recv_sem.at[2])
     ends(mine)
+
+    def late_tile(i):
+        arrived(buf.at[0], recv_sem.at[7 + i])
+
+    def early_block(i):
+        block = buf.at[pl.ds(line * 4, 4)]
+        send(block, block, 5, 1, at(y, 4 + i, line))
+
+    @pl.when(z == 0)
+    def _():
+        for i in (3, 2):
+            late_tile(i)
+            early_block(i)
+        late_tile(1)
+        late_tile(0)
+
+    @pl.when(z == 3)
+    def _():
+        for i in (0, 1):
+            late_tile(i)
+            early_block(i)
+        late_tile(2)
+        late_tile(3)
+
+    @pl.when((z == 1) | (z == 2))
+    def _():
+        for i in range(4):
+            late_tile(i)
+
+    @pl.when(mine == 1)
+    def _():
+        arrived(buf.at[pl.ds(0, 4)], recv_sem.at[1])
+
+    along_x(other, 2, 3)
+    ends(other)
+
     arrange(mine)
     short_transforms(mine)
     frames([(mine * 8 + 1, 6)])
     power([mine * 8 + s for s in range(1, 7)], True)
-
-    arrived(buf.at[pl.ds(0, 4)], recv_sem.at[1])
-    along_x(other, 2, 3)
-    ends(other)
-
-    @pl.when(mine == 0)
-    def _():
-        along_z_far()
 
     arrived(buf.at[pl.ds(0, 28)], recv_sem.at[3])
 
@@ -315,7 +343,18 @@
         out[:, i * WIDTH : i * WIDTH + 256] = total[0:4]
         out[:, i * WIDTH + 256 : (i + 1) * WIDTH] = total[4:8]
 
-    arrived(buf.at[pl.ds(0, 7)], send_sem.at[0])
+    @pl.when(mine == 0)
+    def _():
+        arrived(buf.at[pl.ds(0, 3)], send_sem.at[0])
+
+    @pl.when(mine == 1)
+    def _():
+        arrived(buf.at[pl.ds(0, 7)], send_sem.at[0])
+
+    @pl.when((z == 0) | (z == 3))
+    def _():
+        arrived(buf.at[pl.ds(0, 8)], send_sem.at[5])
+
     arrived(buf.at[pl.ds(0, 28)], send_sem.at[1])
     arrived(buf.at[pl.ds(0, 28)], send_sem.at[2])
 
@@ -361,8 +400,8 @@
             pltpu.VMEM((32, 8, 256), F32),
             pltpu.VMEM((32, 8, 256), F32),
             pltpu.SemaphoreType.DMA((6,)),
-            pltpu.SemaphoreType.DMA((5,)),
-            pltpu.SemaphoreType.DMA((7,)),
+            pltpu.SemaphoreType.DMA((6,)),
+            pltpu.SemaphoreType.DMA((11,)),
         ],
         compiler_params=pltpu.CompilerParams(
             collective_id=0, has_side_effects=True, vmem_limit_bytes=48 * 1024 * 1024

time: 30.5 us -> 27.8 us (0.911); the launches traced: 30.1 us -> 27.7 us
  Pallas kernels: 29.4 us -> 27 us
    pallas_call x1, Pallas kernels: 29.4 us -> 27 us  [body(): pl.pallas_call(kernel, out_shape=jax.ShapeDtypeStruct((4, NFFT), F32), in...]
where the time goes in v3:
time: 27.8 us; the launch traced here: 27.7 us
  Pallas kernels  27 us (97%)
  local copies, waits for them, and re-layouts  0.63 us (2%)
    pallas_call x1, Pallas kernels, body(): pl.pallas_call(kernel, out_shape=jax.ShapeDtypeStruct((4, NFFT), F32), in...  27 us
    unnamed x1, local copies, waits for them, and re-layouts  0.63 us

profile of v3, /device:TPU:1, one launch (start us, length us, event | category | flops | bytes accessed | tf_op | source)
XLA Modules:
  0.0 27.7 jit_solution(18091769194159367871)
XLA Ops:
  0.0 27.0 %shard_map.64 = f32[4,4096]{1,0:T(4,128)S(1)} custom-call(bf16[2,1024]{1,0:T(2,128)(2,1)} %raw_hbm.1, f32[8,128]{1,0:T(8,128)} %bitcast.3, f32[32,128]{1,0:T(8,128)} %bitcast.2, f32[2,16,512]{2,1,0:T(8,128)} %constant.6.clone.step_hbm, f32[8,256,1024]{2,1,0:T(8,128)} %constant.7.clone.channel_hbm, bf16[8,2,512,512]{3,2,1,0:T(8,128)(2,1)} %constant.8.clone.turn_hbm), custom_call_target="tpu_custom_call" | custom-call | tf_op jit(solution)/shard_map/pallas_call | solution.py:380
  27.0 0.6 %copy.8 = f32[4,4096]{1,0:T(4,128)} copy(f32[4,4096]{1,0:T(4,128)S(1)} %shard_map.64) | data formatting | bytes 131072

commit v4 on v3

--- a/solution.py
+++ b/solution.py
@@ -110,6 +110,14 @@
     for i in range(1, PLANES):
         greet(at(ys[i], z, line))
 
+    @pl.when((y > 0) & (line < 7))
+    def _():
+        greet(at(y - 1, z, 7))
+
+    @pl.when((y < PLANES - 1) & (line > 0))
+    def _():
+        greet(at(y + 1, z, 0))
+
     loads[0].wait()
     pair = raw[...].astype(F32)
     for part in range(2):
@@ -129,13 +137,8 @@
     def _():
         halo[1] = jnp.zeros((16, 128), BF16)
 
-    @pl.when(mine == 0)
-    def _():
-        pl.semaphore_wait(barrier, 13)
-
-    @pl.when(mine == 1)
-    def _():
-        pl.semaphore_wait(barrier, 17)
+    sends_ends = ((line == 0) & (y > 0)) | ((line == 7) & (y < PLANES - 1))
+    pl.semaphore_wait(barrier, 13 + 4 * mine + 7 * sends_ends.astype(jnp.int32))
 
     def along_x(part, send_at, recv_at):
         block = buf.at[pl.ds((part * 8 + line) * 4, 4)]
@@ -179,12 +182,7 @@
 
     arrived(buf.at[pl.ds(0, 3)], recv_sem.at[0])
     along_x(mine, 1, 2)
-    for load in loads[3:]:
-        load.wait()
-
-    wins = jnp.concatenate(
-        [window[pl.ds(0, PER_SEG, stride=2), :], window[pl.ds(1, PER_SEG, stride=2), :]], 1
-    ) * (1.0 / 512.0)
+    ends(mine)
     low_rows = lax.broadcasted_iota(jnp.int32, (4, 8, 128), 1) < 4
 
     def arrange(part):
@@ -258,9 +256,6 @@
                 total = term if total is None else total + term
             acc[:, lanes] = total
 
-    arrived(buf.at[pl.ds(0, 28)], recv_sem.at[2])
-    ends(mine)
-
     def late_tile(i):
         arrived(buf.at[0], recv_sem.at[7 + i])
 
@@ -296,6 +291,13 @@
     along_x(other, 2, 3)
     ends(other)
 
+    for load in loads[3:]:
+        load.wait()
+
+    wins = jnp.concatenate(
+        [window[pl.ds(0, PER_SEG, stride=2), :], window[pl.ds(1, PER_SEG, stride=2), :]], 1
+    ) * (1.0 / 512.0)
+    arrived(buf.at[pl.ds(0, 28)], recv_sem.at[2])
     arrange(mine)
     short_transforms(mine)
     frames([(mine * 8 + 1, 6)])

time: 27.8 us -> 26.7 us (0.960)
  Pallas kernels: 27 us -> 25.9 us
    pallas_call x1, Pallas kernels: 27 us -> 25.9 us  [body(): pl.pallas_call(kernel, out_shape=jax.ShapeDtypeStruct((4, NFFT), F32), in...]
where the time goes in v4:
time: 26.7 us; the launch traced here: 26.5 us
  Pallas kernels  25.9 us (97%)
  local copies, waits for them, and re-layouts  0.63 us (2%)
    pallas_call x1, Pallas kernels, body(): pl.pallas_call(kernel, out_shape=jax.ShapeDtypeStruct((4, NFFT), F32), in...  25.9 us
    unnamed x1, local copies, waits for them, and re-layouts  0.63 us

profile of v4, /device:TPU:1, one launch (start us, length us, event | category | flops | bytes accessed | tf_op | source)
XLA Modules:
  0.0 26.5 jit_solution(4250757338170765055)
XLA Ops:
  0.0 25.9 %shard_map.64 = f32[4,4096]{1,0:T(4,128)S(1)} custom-call(bf16[2,1024]{1,0:T(2,128)(2,1)} %raw_hbm.1, f32[8,128]{1,0:T(8,128)} %bitcast.3, f32[32,128]{1,0:T(8,128)} %bitcast.2, f32[2,16,512]{2,1,0:T(8,128)} %constant.6.clone.step_hbm, f32[8,256,1024]{2,1,0:T(8,128)} %constant.7.clone.channel_hbm, bf16[8,2,512,512]{3,2,1,0:T(8,128)(2,1)} %constant.8.clone.turn_hbm), custom_call_target="tpu_custom_call" | custom-call | tf_op jit(solution)/shard_map/pallas_call | solution.py:382
  25.9 0.6 %copy.8 = f32[4,4096]{1,0:T(4,128)} copy(f32[4,4096]{1,0:T(4,128)S(1)} %shard_map.64) | data formatting | bytes 131072

commit v5 on v4

--- a/solution.py
+++ b/solution.py
@@ -53,7 +53,7 @@
 def kernel(
     raw_hbm, taper_hbm, window_hbm, step_hbm, channel_hbm, turn_hbm, out,
     raw, taper, window, tile32, buf, halo, rows32, coef32, coef, turn, step, lhs, rhs, acc, blocks, landed,
-    local_sem, send_sem, recv_sem,
+    local_sem, send_sem, recv_sem, known,
 ):
     tm, grp = lax.axis_index("tm"), lax.axis_index("grp")
     y, z, x_lo = tm // 16, lax.rem(tm // 2, DEPTH), lax.rem(tm, 2)
@@ -93,6 +93,7 @@
     loads[0].start()
 
     barrier = pltpu.get_barrier_semaphore()
+    even_core, odd_core = line - core, line - core + 1
 
     def greet(to):
         pl.semaphore_signal(barrier, inc=1, device_id=to, device_id_type=MESH)
@@ -100,23 +101,42 @@
     @pl.when(mine == 0)
     def _():
         for i in range(4):
-            greet(at(y, 4 + i, line))
-
-    for i in range(1, 4):
-        greet(at(y, mine * 4 + lax.rem(zz + i, 4), line))
-
-    for dx, dc in MEMBERS:
-        greet(at(y, z, member(dx, dc)))
-    for i in range(1, PLANES):
-        greet(at(ys[i], z, line))
-
-    @pl.when((y > 0) & (line < 7))
-    def _():
-        greet(at(y - 1, z, 7))
-
-    @pl.when((y < PLANES - 1) & (line > 0))
-    def _():
-        greet(at(y + 1, z, 0))
+            greet(at(y, 4 + i, even_core))
+        for i in range(1, 4):
+            greet(at(y, lax.rem(zz + i, 4), line))
+        for dx, dc in MEMBERS:
+            greet(at(y, z, member(dx, dc)))
+        for i in range(1, PLANES):
+            greet(at(ys[i], z, line))
+
+        @pl.when((y > 0) & (line < 7))
+        def _():
+            greet(at(y - 1, z, 7))
+
+        @pl.when((y < PLANES - 1) & (line > 0))
+        def _():
+            greet(at(y + 1, z, 0))
+
+    @pl.when(mine == 1)
+    def _():
+        @pl.when(core == 1)
+        def _():
+            greet(at(y, z, even_core))
+
+        for i in range(1, 4):
+            greet(at(y, 4 + lax.rem(zz + i, 4), odd_core))
+        for dx in (2, 1, 3):
+            greet(at(y, z, lax.rem(xs[dx], 2) * 4 + xs[dx] // 2 * 2 + 1))
+        for i in range(1, PLANES):
+            greet(at(ys[i], z, odd_core))
+
+        @pl.when((y > 0) & (line < 6))
+        def _():
+            greet(at(y - 1, z, 7))
+
+        @pl.when((y < PLANES - 1) & (line > 1))
+        def _():
+            greet(at(y + 1, z, 1))
 
     loads[0].wait()
     pair = raw[...].astype(F32)
@@ -137,8 +157,35 @@
     def _():
         halo[1] = jnp.zeros((16, 128), BF16)
 
-    sends_ends = ((line == 0) & (y > 0)) | ((line == 7) & (y < PLANES - 1))
-    pl.semaphore_wait(barrier, 13 + 4 * mine + 7 * sends_ends.astype(jnp.int32))
+    partner = at(y, z, member(0, 1))
+    last, first = (line == 7) & (y < PLANES - 1), y > 0
+
+    @pl.when(mine == 0)
+    def _():
+        pl.semaphore_wait(barrier, 13 + 7 * (last | ((line == 0) & first)).astype(jnp.int32))
+
+    @pl.when((mine == 1) & (core == 0))
+    def _():
+        pl.semaphore_wait(barrier, 9)
+        pl.semaphore_signal(known.at[0], inc=1, device_id=partner, device_id_type=MESH)
+
+    @pl.when((mine == 1) & (core == 1))
+    def _():
+        pl.semaphore_wait(known.at[0], 1)
+
+    @pl.when(mine == 1)
+    def _():
+        for i in range(4):
+            send(buf.at[own], buf.at[own], 0, 7 + zz, at(y, i, line))
+
+    @pl.when((mine == 1) & (core == 1))
+    def _():
+        pl.semaphore_wait(barrier, 18 + 6 * (last | ((line == 1) & first)).astype(jnp.int32))
+        pl.semaphore_signal(known.at[1], inc=1, device_id=partner, device_id_type=MESH)
+
+    @pl.when((mine == 1) & (core == 0))
+    def _():
+        pl.semaphore_wait(known.at[1], 1)
 
     def along_x(part, send_at, recv_at):
         block = buf.at[pl.ds((part * 8 + line) * 4, 4)]
@@ -155,11 +202,6 @@
         def _():
             for i in range(8):
                 send(buf.at[63], halo.at[0], 3, 4, at(y + 1, z, i))
-
-    @pl.when(mine == 1)
-    def _():
-        for i in range(4):
-            send(buf.at[own], buf.at[own], 0, 7 + zz, at(y, i, line))
 
     for i in range(1, 4):
         send(buf.at[own], buf.at[own], 0, 0, at(y, mine * 4 + lax.rem(zz + i, 4), line))
@@ -404,6 +446,7 @@
             pltpu.SemaphoreType.DMA((6,)),
             pltpu.SemaphoreType.DMA((6,)),
             pltpu.SemaphoreType.DMA((11,)),
+            pltpu.SemaphoreType.REGULAR((2,)),
         ],
         compiler_params=pltpu.CompilerParams(
             collective_id=0, has_side_effects=True, vmem_limit_bytes=48 * 1024 * 1024

time: 26.7 us -> 25.9 us (0.970)
  Pallas kernels: 25.9 us -> 25.1 us
    pallas_call x1, Pallas kernels: 25.9 us -> 25.1 us  [body(): pl.pallas_call(kernel, out_shape=jax.ShapeDtypeStruct((4, NFFT), F32), in...]
where the time goes in v5:
time: 25.9 us; the launch traced here: 25.7 us
  Pallas kernels  25.1 us (97%)
  local copies, waits for them, and re-layouts  0.63 us (2%)
    pallas_call x1, Pallas kernels, body(): pl.pallas_call(kernel, out_shape=jax.ShapeDtypeStruct((4, NFFT), F32), in...  25.1 us
    unnamed x1, local copies, waits for them, and re-layouts  0.63 us

profile of v5, /device:TPU:1, one launch (start us, length us, event | category | flops | bytes accessed | tf_op | source)
XLA Modules:
  0.0 25.7 jit_solution(9455816474887891081)
XLA Ops:
  0.0 25.1 %shard_map.64 = f32[4,4096]{1,0:T(4,128)S(1)} custom-call(bf16[2,1024]{1,0:T(2,128)(2,1)} %raw_hbm.1, f32[8,128]{1,0:T(8,128)} %bitcast.3, f32[32,128]{1,0:T(8,128)} %bitcast.2, f32[2,16,512]{2,1,0:T(8,128)} %constant.6.clone.step_hbm, f32[8,256,1024]{2,1,0:T(8,128)} %constant.7.clone.channel_hbm, bf16[8,2,512,512]{3,2,1,0:T(8,128)(2,1)} %constant.8.clone.turn_hbm), custom_call_target="tpu_custom_call" | custom-call | tf_op jit(solution)/shard_map/pallas_call | solution.py:424
  25.1 0.6 %copy.8 = f32[4,4096]{1,0:T(4,128)} copy(f32[4,4096]{1,0:T(4,128)S(1)} %shard_map.64) | data formatting | bytes 131072

commit v6 on v5

--- a/solution.py
+++ b/solution.py
@@ -25,6 +25,7 @@
 WIDTH = NFFT // LINE
 HOPS = (0, 1, 2, 1)
 MEMBERS = sorted(((dx, dc) for dx in range(4) for dc in range(2) if dx or dc), key=lambda m: -HOPS[m[0]])
+FIRST = 1
 OWNERS = sorted(
     ((dy, dx, dc) for dy in range(4) for dx in range(4) for dc in range(2) if dy or dx or dc),
     key=lambda m: -(HOPS[m[0]] + HOPS[m[1]]),
@@ -341,8 +342,8 @@
     ) * (1.0 / 512.0)
     arrived(buf.at[pl.ds(0, 28)], recv_sem.at[2])
     arrange(mine)
+    frames([(mine * 8 + 1, 6)])
     short_transforms(mine)
-    frames([(mine * 8 + 1, 6)])
     power([mine * 8 + s for s in range(1, 7)], True)
 
     arrived(buf.at[pl.ds(0, 28)], recv_sem.at[3])
@@ -363,8 +364,8 @@
         rows32[8 + ROWS : 9 + ROWS, lane : lane + 128] = after[p * 8 : p * 8 + 1]
         rows32[8 + ROWS : 9 + ROWS, lane + 128 : lane + 256] = after[p * 8 + 4 : p * 8 + 5]
     arrange(other)
+    frames([(mine * 8, 1), (mine * 8 + 7, 1), (other * 8, 8)])
     short_transforms(other)
-    frames([(mine * 8, 1), (mine * 8 + 7, 1), (other * 8, 8)])
     power([mine * 8, mine * 8 + 7] + [other * 8 + s for s in range(8)], False)
 
     low_half = lax.broadcasted_iota(jnp.int32, (16, 8, 256), 1) < 4
@@ -376,16 +377,30 @@
         blocks[2 * t] = even[t]
         blocks[2 * t + 1] = odd[t]
 
+    def serve(to, sem):
+        send(blocks.at[to], landed.at[place], 4, sem, at(to // 8, z, lax.rem(to, 8)))
+
+    @pl.when(place != FIRST)
+    def _():
+        serve(FIRST, 11 + y)
+
     for dy, dx, dc in OWNERS:
         to = ys[dy] * 8 + member(dx, dc)
-        send(blocks.at[to], landed.at[place], 4, 6, at(ys[dy], z, member(dx, dc)))
+
+        @pl.when(to != FIRST)
+        def _():
+            serve(to, 11 + y)
 
     landed[place] = blocks[place]
-    arrived(landed.at[pl.ds(0, 31)], recv_sem.at[6])
+    totals = [None] * LINE
+    for dy in (0, 1, 3, 2):
+        arrived(landed.at[pl.ds(0, 8 if dy else 7)], recv_sem.at[11 + ys[dy]])
+        for i in range(LINE):
+            block = landed[ys[dy] * 8 + i]
+            totals[i] = block if dy == 0 else totals[i] + block
     for i in range(LINE):
-        total = landed[i] + landed[8 + i] + landed[16 + i] + landed[24 + i]
-        out[:, i * WIDTH : i * WIDTH + 256] = total[0:4]
-        out[:, i * WIDTH + 256 : (i + 1) * WIDTH] = total[4:8]
+        out[:, i * WIDTH : i * WIDTH + 256] = totals[i][0:4]
+        out[:, i * WIDTH + 256 : (i + 1) * WIDTH] = totals[i][4:8]
 
     @pl.when(mine == 0)
     def _():
@@ -445,7 +460,7 @@
             pltpu.VMEM((32, 8, 256), F32),
             pltpu.SemaphoreType.DMA((6,)),
             pltpu.SemaphoreType.DMA((6,)),
-            pltpu.SemaphoreType.DMA((11,)),
+            pltpu.SemaphoreType.DMA((15,)),
             pltpu.SemaphoreType.REGULAR((2,)),
         ],
         compiler_params=pltpu.CompilerParams(

time: 25.9 us -> 25.2 us (0.973)
  Pallas kernels: 25.1 us -> 24.4 us
    pallas_call x1, Pallas kernels: 25.1 us -> 24.4 us  [body(): pl.pallas_call(kernel, out_shape=jax.ShapeDtypeStruct((4, NFFT), F32), in...]
where the time goes in v6:
time: 25.2 us; the launch traced here: 25.1 us
  Pallas kernels  24.4 us (97%)
  local copies, waits for them, and re-layouts  0.63 us (2%)
    pallas_call x1, Pallas kernels, body(): pl.pallas_call(kernel, out_shape=jax.ShapeDtypeStruct((4, NFFT), F32), in...  24.4 us
    unnamed x1, local copies, waits for them, and re-layouts  0.63 us

profile of v6, /device:TPU:1, one launch (start us, length us, event | category | flops | bytes accessed | tf_op | source)
XLA Modules:
  0.0 25.1 jit_solution(12357236463207309349)
XLA Ops:
  0.0 24.4 %shard_map.64 = f32[4,4096]{1,0:T(4,128)S(1)} custom-call(bf16[2,1024]{1,0:T(2,128)(2,1)} %raw_hbm.1, f32[8,128]{1,0:T(8,128)} %bitcast.3, f32[32,128]{1,0:T(8,128)} %bitcast.2, f32[2,16,512]{2,1,0:T(8,128)} %constant.6.clone.step_hbm, f32[8,256,1024]{2,1,0:T(8,128)} %constant.7.clone.channel_hbm, bf16[8,2,512,512]{3,2,1,0:T(8,128)(2,1)} %constant.8.clone.turn_hbm), custom_call_target="tpu_custom_call" | custom-call | tf_op jit(solution)/shard_map/pallas_call | solution.py:439
  24.4 0.6 %copy.8 = f32[4,4096]{1,0:T(4,128)} copy(f32[4,4096]{1,0:T(4,128)S(1)} %shard_map.64) | data formatting | bytes 131072

commit v7 on v6

--- a/solution.py
+++ b/solution.py
@@ -26,10 +26,6 @@
 HOPS = (0, 1, 2, 1)
 MEMBERS = sorted(((dx, dc) for dx in range(4) for dc in range(2) if dx or dc), key=lambda m: -HOPS[m[0]])
 FIRST = 1
-OWNERS = sorted(
-    ((dy, dx, dc) for dy in range(4) for dx in range(4) for dc in range(2) if dy or dx or dc),
-    key=lambda m: -(HOPS[m[0]] + HOPS[m[1]]),
-)
 
 
 def tables():
@@ -103,6 +99,12 @@
     def _():
         for i in range(4):
             greet(at(y, 4 + i, even_core))
+
+        @pl.when(z == 0)
+        def _():
+            for i in range(4):
+                greet(at(y, 4 + i, lax.rem(xs[2], 2) * 4 + xs[2] // 2 * 2))
+
         for i in range(1, 4):
             greet(at(y, lax.rem(zz + i, 4), line))
         for dx, dc in MEMBERS:
@@ -167,7 +169,7 @@
 
     @pl.when((mine == 1) & (core == 0))
     def _():
-        pl.semaphore_wait(barrier, 9)
+        pl.semaphore_wait(barrier, 11)
         pl.semaphore_signal(known.at[0], inc=1, device_id=partner, device_id_type=MESH)
 
     @pl.when((mine == 1) & (core == 1))
@@ -176,6 +178,8 @@
 
     @pl.when(mine == 1)
     def _():
+        for dc in range(2):
+            send(buf.at[own], buf.at[own], 0, 3, at(y, 0, member(2, dc)))
         for i in range(4):
             send(buf.at[own], buf.at[own], 0, 7 + zz, at(y, i, line))
 
@@ -188,9 +192,9 @@
     def _():
         pl.semaphore_wait(known.at[1], 1)
 
-    def along_x(part, send_at, recv_at):
+    def along_x(part, send_at, recv_at, members):
         block = buf.at[pl.ds((part * 8 + line) * 4, 4)]
-        for dx, dc in MEMBERS:
+        for dx, dc in members:
             send(block, block, send_at, recv_at, at(y, z, member(dx, dc)))
 
     def ends(part):
@@ -224,7 +228,7 @@
             coef[a, STRIP:, 256 + h * 128 : 256 + (h + 1) * 128] = cosine
 
     arrived(buf.at[pl.ds(0, 3)], recv_sem.at[0])
-    along_x(mine, 1, 2)
+    along_x(mine, 1, 2, MEMBERS)
     ends(mine)
     low_rows = lax.broadcasted_iota(jnp.int32, (4, 8, 128), 1) < 4
 
@@ -331,7 +335,11 @@
     def _():
         arrived(buf.at[pl.ds(0, 4)], recv_sem.at[1])
 
-    along_x(other, 2, 3)
+    @pl.when(z > 0)
+    def _():
+        along_x(other, 2, 3, MEMBERS[:2])
+
+    along_x(other, 2, 3, MEMBERS[2:])
     ends(other)
 
     for load in loads[3:]:
@@ -366,30 +374,41 @@
     arrange(other)
     frames([(mine * 8, 1), (mine * 8 + 7, 1), (other * 8, 8)])
     short_transforms(other)
-    power([mine * 8, mine * 8 + 7] + [other * 8 + s for s in range(8)], False)
-
-    low_half = lax.broadcasted_iota(jnp.int32, (16, 8, 256), 1) < 4
-    left = acc[:, :256].reshape(16, 8, 256)
-    right = acc[:, 256:].reshape(16, 8, 256)
-    even = jnp.where(low_half, left, pltpu.roll(right, 4, 1))
-    odd = jnp.where(low_half, pltpu.roll(left, 4, 1), right)
-    for t in range(16):
-        blocks[2 * t] = even[t]
-        blocks[2 * t + 1] = odd[t]
-
-    def serve(to, sem):
-        send(blocks.at[to], landed.at[place], 4, sem, at(to // 8, z, lax.rem(to, 8)))
-
-    @pl.when(place != FIRST)
-    def _():
-        serve(FIRST, 11 + y)
-
-    for dy, dx, dc in OWNERS:
-        to = ys[dy] * 8 + member(dx, dc)
-
-        @pl.when(to != FIRST)
-        def _():
-            serve(to, 11 + y)
+    rest = [mine * 8, mine * 8 + 7] + [other * 8 + s for s in range(8)]
+    low_half = lax.broadcasted_iota(jnp.int32, (4, 8, 256), 1) < 4
+
+    def serve(to):
+        send(blocks.at[to], landed.at[place], 4, 11 + y, at(to // 8, z, lax.rem(to, 8)))
+
+    for c in (0, 32, 64, 96):
+        lefts = []
+        for n in range(2):
+            lanes = slice(n * 256, (n + 1) * 256)
+            total = acc[c : c + 32, lanes]
+            for s in rest:
+                pair = jnp.concatenate([lhs[s, c : c + 32], lhs[s, STRIP + c : STRIP + c + 32]], 0)
+                e = jnp.dot(pair, rhs[s][:, lanes], preferred_element_type=F32)
+                total = total + (e[:32] * e[:32] + e[32:] * e[32:])
+            lefts.append(total.reshape(4, 8, 256))
+        left, right = lefts
+        even = jnp.where(low_half, left, pltpu.roll(right, 4, 1))
+        odd = jnp.where(low_half, pltpu.roll(left, 4, 1), right)
+        for t in range(4):
+            blocks[c // 4 + 2 * t] = even[t]
+            blocks[c // 4 + 2 * t + 1] = odd[t]
+
+        if c == 0:
+
+            @pl.when(place != FIRST)
+            def _():
+                serve(FIRST)
+
+        for dx, dc in MEMBERS + [(0, 0)]:
+            to = c // 4 + member(dx, dc)
+
+            @pl.when((to != FIRST) & (to != place))
+            def _(to=to):
+                serve(to)
 
     landed[place] = blocks[place]
     totals = [None] * LINE
@@ -408,14 +427,22 @@
 
     @pl.when(mine == 1)
     def _():
-        arrived(buf.at[pl.ds(0, 7)], send_sem.at[0])
+        arrived(buf.at[pl.ds(0, 9)], send_sem.at[0])
 
     @pl.when((z == 0) | (z == 3))
     def _():
         arrived(buf.at[pl.ds(0, 8)], send_sem.at[5])
 
     arrived(buf.at[pl.ds(0, 28)], send_sem.at[1])
-    arrived(buf.at[pl.ds(0, 28)], send_sem.at[2])
+
+    @pl.when(z == 0)
+    def _():
+        arrived(buf.at[pl.ds(0, 20)], send_sem.at[2])
+
+    @pl.when(z > 0)
+    def _():
+        arrived(buf.at[pl.ds(0, 28)], send_sem.at[2])
+
 
     @pl.when((line == 0) & (y > 0))
     def _():

time: 25.2 us -> 24.2 us (0.960)
  Pallas kernels: 24.4 us -> 23.4 us
    pallas_call x1, Pallas kernels: 24.4 us -> 23.4 us  [body(): pl.pallas_call(kernel, out_shape=jax.ShapeDtypeStruct((4, NFFT), F32), in...]
where the time goes in v7:
time: 24.2 us; the launch traced here: 24 us
  Pallas kernels  23.4 us (97%)
  local copies, waits for them, and re-layouts  0.63 us (3%)
    pallas_call x1, Pallas kernels, body(): pl.pallas_call(kernel, out_shape=jax.ShapeDtypeStruct((4, NFFT), F32), in...  23.4 us
    unnamed x1, local copies, waits for them, and re-layouts  0.63 us

profile of v7, /device:TPU:1, one launch (start us, length us, event | category | flops | bytes accessed | tf_op | source)
XLA Modules:
  0.0 24.0 jit_solution(6235535519636758587)
XLA Ops:
  0.0 23.4 %shard_map.64 = f32[4,4096]{1,0:T(4,128)S(1)} custom-call(bf16[2,1024]{1,0:T(2,128)(2,1)} %raw_hbm.1, f32[8,128]{1,0:T(8,128)} %bitcast.3, f32[32,128]{1,0:T(8,128)} %bitcast.2, f32[2,16,512]{2,1,0:T(8,128)} %constant.6.clone.step_hbm, f32[8,256,1024]{2,1,0:T(8,128)} %constant.7.clone.channel_hbm, bf16[8,2,512,512]{3,2,1,0:T(8,128)(2,1)} %constant.8.clone.turn_hbm), custom_call_target="tpu_custom_call" | custom-call | tf_op jit(solution)/shard_map/pallas_call | solution.py:466
  23.4 0.6 %copy.8 = f32[4,4096]{1,0:T(4,128)} copy(f32[4,4096]{1,0:T(4,128)S(1)} %shard_map.64) | data formatting | bytes 131072

commit v8 on v7

--- a/solution.py
+++ b/solution.py
@@ -141,6 +141,13 @@
         def _():
             greet(at(y + 1, z, 1))
 
+    partner = at(y, z, member(0, 1))
+
+    @pl.when((mine == 1) & (core == 0))
+    def _():
+        pl.semaphore_wait(barrier, 11)
+        pl.semaphore_signal(known.at[0], inc=1, device_id=partner, device_id_type=MESH)
+
     loads[0].wait()
     pair = raw[...].astype(F32)
     for part in range(2):
@@ -160,17 +167,11 @@
     def _():
         halo[1] = jnp.zeros((16, 128), BF16)
 
-    partner = at(y, z, member(0, 1))
     last, first = (line == 7) & (y < PLANES - 1), y > 0
 
     @pl.when(mine == 0)
     def _():
         pl.semaphore_wait(barrier, 13 + 7 * (last | ((line == 0) & first)).astype(jnp.int32))
-
-    @pl.when((mine == 1) & (core == 0))
-    def _():
-        pl.semaphore_wait(barrier, 11)
-        pl.semaphore_signal(known.at[0], inc=1, device_id=partner, device_id_type=MESH)
 
     @pl.when((mine == 1) & (core == 1))
     def _():
@@ -339,7 +340,14 @@
     def _():
         along_x(other, 2, 3, MEMBERS[:2])
 
-    along_x(other, 2, 3, MEMBERS[2:])
+    @pl.when(core == 0)
+    def _():
+        along_x(other, 2, 3, sorted(MEMBERS[2:], key=lambda m: (m[0] == 0, -m[1], -m[0])))
+
+    @pl.when(core == 1)
+    def _():
+        along_x(other, 2, 3, sorted(MEMBERS[2:], key=lambda m: (m[0] == 0, m[1], -m[0])))
+
     ends(other)
 
     for load in loads[3:]:

time: 24.2 us -> 24.5 us (1.012)
  Pallas kernels: 23.4 us -> 23.7 us
    pallas_call x1, Pallas kernels: 23.4 us -> 23.7 us  [body(): pl.pallas_call(kernel, out_shape=jax.ShapeDtypeStruct((4, NFFT), F32), in...]
where the time goes in v8:
time: 24.5 us; the launch traced here: 24.3 us
  Pallas kernels  23.7 us (97%)
  local copies, waits for them, and re-layouts  0.63 us (3%)
    pallas_call x1, Pallas kernels, body(): pl.pallas_call(kernel, out_shape=jax.ShapeDtypeStruct((4, NFFT), F32), in...  23.7 us
    unnamed x1, local copies, waits for them, and re-layouts  0.63 us

profile of v8, /device:TPU:1, one launch (start us, length us, event | category | flops | bytes accessed | tf_op | source)
XLA Modules:
  0.0 24.3 jit_solution(2254798684448522259)
XLA Ops:
  0.0 23.7 %shard_map.64 = f32[4,4096]{1,0:T(4,128)S(1)} custom-call(bf16[2,1024]{1,0:T(2,128)(2,1)} %raw_hbm.1, f32[8,128]{1,0:T(8,128)} %bitcast.3, f32[32,128]{1,0:T(8,128)} %bitcast.2, f32[2,16,512]{2,1,0:T(8,128)} %constant.6.clone.step_hbm, f32[8,256,1024]{2,1,0:T(8,128)} %constant.7.clone.channel_hbm, bf16[8,2,512,512]{3,2,1,0:T(8,128)(2,1)} %constant.8.clone.turn_hbm), custom_call_target="tpu_custom_call" | custom-call | tf_op jit(solution)/shard_map/pallas_call | solution.py:474
  23.7 0.6 %copy.8 = f32[4,4096]{1,0:T(4,128)} copy(f32[4,4096]{1,0:T(4,128)S(1)} %shard_map.64) | data formatting | bytes 131072
